TPU v7x, 128 devices: a whole 4x4x4 slice. The times are simulated.
128 devices in a mesh: seq: 8 (over y_lo, z), ctx: 16 (over y_hi, x, core).
Axes of the slice: x: 4, y: 4 (y_hi: 2, y_lo: 2; y = y_hi * 2 + y_lo), z: 4, core: 2. Of those that a mesh axis runs over, the one named last changes fastest.
Arguments:
- tokens: bfloat16 [16384, 1152], P(('seq', 'ctx')), may hold values from -6 to 6
- prefix_len: int32 [8], P('seq'), may hold values from 204 to 1024
- query_weight: bfloat16 [1152, 1024], P(('seq', 'ctx')), may hold values from -0.5 to 0.5
- key_weight: bfloat16 [1152, 256], P(('seq', 'ctx')), may hold values from -0.1875 to 0.1875
- value_weight: bfloat16 [1152, 256], P(('seq', 'ctx')), may hold values from -0.1875 to 0.1875
- mixing_weight: bfloat16 [1024, 1152], P(('seq', 'ctx')), may hold values from -0.1875 to 0.1875
- gate_weight: bfloat16 [1152, 6912], P(('seq', 'ctx')), may hold values from -0.1875 to 0.1875
- up_weight: bfloat16 [1152, 6912], P(('seq', 'ctx')), may hold values from -0.1875 to 0.1875
- down_weight: bfloat16 [6912, 1152], P(('seq', 'ctx')), may hold values from -0.078125 to 0.078125
- entry_gain: bfloat16 [1152], P(('seq', 'ctx')), may hold values from 0.5 to 1.5
- mixed_gain: bfloat16 [1152], P(('seq', 'ctx')), may hold values from 0.5 to 1.5
- middle_gain: bfloat16 [1152], P(('seq', 'ctx')), may hold values from 0.5 to 1.5
- closing_gain: bfloat16 [1152], P(('seq', 'ctx')), may hold values from 0.5 to 1.5
- cotangent: bfloat16 [16384, 1152], P(('seq', 'ctx')), may hold values from -6 to 6
Outputs:
- layer_output: bfloat16 [16384, 1152], P(('seq', 'ctx'))
- input_delta: float32 [16384, 1152], P(('seq', 'ctx'))
- query_delta: float32 [1152, 1024], P(('seq', 'ctx'))
- key_delta: float32 [1152, 256], P(('seq', 'ctx'))
- value_delta: float32 [1152, 256], P(('seq', 'ctx'))
- mixing_delta: float32 [1024, 1152], P(('seq', 'ctx'))
- gate_delta: float32 [1152, 6912], P(('seq', 'ctx'))
- up_delta: float32 [1152, 6912], P(('seq', 'ctx'))
- down_delta: float32 [6912, 1152], P(('seq', 'ctx'))
- entry_delta: float32 [1152], P(('seq', 'ctx'))
- mixed_delta: float32 [1152], P(('seq', 'ctx'))
- middle_delta: float32 [1152], P(('seq', 'ctx'))
- closing_delta: float32 [1152], P(('seq', 'ctx'))
All inputs are finite; a program needn't handle non-finite values.
Results may differ from a plain program's by a relative error of at most 0.025.
Values may be sent and summed in bfloat16 or wider, within the bound.
No kernel may reach another device: no remote copies, remote signals or barrier semaphores. Data moves between devices by JAX's collectives and lax.ppermute only.
A program may use at most 128 MiB of HBM per device.

v0:
```python
import jax
import jax.numpy as jnp
from jax import lax
from jax.sharding import PartitionSpec as P

EPS = 1e-06
CAP = 20.0
QSCALE = 0.0625
THETA = 1000000.0


def sent_together(arrays, axis, split_dim, concat_dim, along):
    ends, at = ([], 0)
    for a in arrays[:-1]:
        at += a.shape[along]
        ends.append(at)
    both = jnp.concatenate(arrays, axis=along)
    return tuple(
        jnp.split(
            lax.all_to_all(both, axis, split_axis=split_dim, concat_axis=concat_dim, tiled=True),
            ends,
            axis=along,
        )
    )


def side_by_side(arrays, axis, dim, along):
    both = jnp.concatenate(arrays, axis=along)
    filled, at, gathered = (lax.all_gather(both, axis, axis=dim, tiled=True), 0, [])
    for a in arrays:
        gathered.append(lax.slice_in_dim(filled, at, at + a.shape[along], axis=along))
        at += a.shape[along]
    return tuple(gathered)


def side_by_side_2(arrays, axis, dim, along):
    widths = [a.shape[along] for a in arrays]
    both = jnp.concatenate(arrays, axis=along)
    filled = lax.psum_scatter(both, axis, scatter_dimension=dim, tiled=True)
    return tuple(jnp.split(filled, [sum(widths[:k]) for k in range(1, len(widths))], axis=along))


def in_blocks(shard, dim, peers):
    before, after = (shard.shape[:dim], shard.shape[dim + 1 :])
    return jnp.moveaxis(shard.reshape(*before, peers, -1, *after), dim, 0)


def sum_together(arrays, axis, dims):
    peers = lax.axis_size(axis)
    parts = [in_blocks(a, dim, peers) for a, dim in zip(arrays, dims)]
    lines = jnp.concatenate([b.reshape(peers, -1) for b in parts], axis=1)
    rows = max(16, -(-lines.shape[1] // 1024) * 8)
    lines = jnp.pad(lines, ((0, 0), (0, rows * 128 - lines.shape[1]))).reshape(-1, 128)
    vector, at, gathered = (lax.psum_scatter(lines, axis, tiled=True).reshape(-1), 0, [])
    for b in parts:
        part = b[0]
        gathered.append(vector[at : at + part.size].reshape(part.shape))
        at += part.size
    return tuple(gathered)


def rms_scale(values, gain):
    return values * lax.rsqrt(jnp.mean(values * values, axis=-1, keepdims=True) + EPS) * gain


def rotate(values, angles):
    half = values.shape[-1] // 2
    first = values[..., :half]
    second = values[..., half:]
    cosine = jnp.cos(angles)
    sine = jnp.sin(angles)
    return jnp.concatenate(
        [first * cosine - second * sine, second * cosine + first * sine], axis=-1
    )


def outer(left, right):
    return lax.dot_general(
        left, right, (((0,), (0,)), ((), ())), preferred_element_type=jnp.float32
    )


def through(left, weight):
    return lax.dot_general(
        left, weight, (((1,), (1,)), ((), ())), preferred_element_type=jnp.float32
    )


def product(left, right):
    return jnp.dot(left, right, preferred_element_type=jnp.float32)


def gated(gate, up):
    return jax.nn.gelu(gate, approximate=True) * up


def fetch_columns(gate_weight, up_weight, down_weight):
    seq_count = lax.axis_size("seq")
    ctx_count = lax.axis_size("ctx")
    row_block = gate_weight.shape[0]
    unit_block = gate_weight.shape[1] // (seq_count * ctx_count)
    gate_split = gate_weight.reshape(row_block, seq_count, ctx_count, unit_block)
    up_split = up_weight.reshape(row_block, seq_count, ctx_count, unit_block)
    gate_swapped, up_swapped = sent_together((gate_split, up_split), "ctx", 2, 0, 1)
    gate_rows, up_rows, down_rows = (
        *side_by_side((gate_swapped, up_swapped), "seq", 0, 1),
        lax.all_gather(down_weight, "seq", axis=0, tiled=True),
    )
    width = gate_rows.shape[0]
    return (gate_rows.reshape(width, -1), up_rows.reshape(width, -1), down_rows)


def return_columns(gate_term, up_term, down_term):
    seq_count = lax.axis_size("seq")
    width = gate_term.shape[0]
    unit_block = gate_term.shape[1] // seq_count
    gate_split = gate_term.reshape(width, seq_count, 1, unit_block)
    up_split = up_term.reshape(width, seq_count, 1, unit_block)
    gate_sum, up_sum, down_sum = (
        *tuple(
            (
                part.astype(jnp.float32)
                for part in side_by_side_2(
                    (gate_split.astype(jnp.bfloat16), up_split.astype(jnp.bfloat16)), "seq", 0, 1
                )
            )
        ),
        lax.psum_scatter(
            down_term.astype(jnp.bfloat16), "seq", scatter_dimension=0, tiled=True
        ).astype(jnp.float32),
    )
    gate_owned, up_owned = tuple(
        (
            part.astype(jnp.float32)
            for part in sent_together(
                (gate_sum.astype(jnp.bfloat16), up_sum.astype(jnp.bfloat16)), "ctx", 0, 2, 1
            )
        )
    )
    rows = gate_owned.shape[0]
    return (gate_owned.reshape(rows, -1), up_owned.reshape(rows, -1), down_sum)


def body(
    tokens,
    prefix_len,
    query_weight,
    key_weight,
    value_weight,
    mixing_weight,
    gate_weight,
    up_weight,
    down_weight,
    entry_gain,
    mixed_gain,
    middle_gain,
    closing_gain,
    cotangent,
):
    count = tokens.shape[0]
    head = key_weight.shape[1]
    heads = query_weight.shape[1] // head
    half = head // 2
    length = count * lax.axis_size("ctx")
    offset = lax.axis_index("ctx") * count
    query_pos = offset + jnp.arange(count, dtype=jnp.int32)
    key_pos = jnp.arange(length, dtype=jnp.int32)
    allowed = (key_pos[None, :] <= query_pos[:, None]) | (key_pos[None, :] < prefix_len[0])
    inverse = 1.0 / THETA ** (jnp.arange(half, dtype=jnp.float32) * (2.0 / head))
    angles = query_pos.astype(jnp.float32)[:, None] * inverse[None, :]
    inputs = tokens.astype(jnp.float32)
    (
        query_full,
        key_full,
        value_full,
        mixing_full,
        entry_full,
        mixed_full,
        middle_full,
        closing_full,
    ) = (
        *side_by_side((query_weight, key_weight, value_weight), ("seq", "ctx"), 0, 1),
        lax.all_gather(mixing_weight, ("seq", "ctx"), axis=0, tiled=True),
        lax.all_gather(entry_gain, ("seq", "ctx"), axis=0, tiled=True),
        lax.all_gather(mixed_gain, ("seq", "ctx"), axis=0, tiled=True),
        lax.all_gather(middle_gain, ("seq", "ctx"), axis=0, tiled=True),
        lax.all_gather(closing_gain, ("seq", "ctx"), axis=0, tiled=True),
    )
    entry_scale = entry_full.astype(jnp.float32)
    mixed_scale = mixed_full.astype(jnp.float32)
    middle_scale = middle_full.astype(jnp.float32)
    closing_scale = closing_full.astype(jnp.float32)
    entry_in = rms_scale(inputs, entry_scale).astype(jnp.bfloat16)
    query_raw = product(entry_in, query_full)
    key_raw = product(entry_in, key_full)
    value_raw = product(entry_in, value_full)
    queries = (rotate(query_raw.reshape(count, heads, head), angles[:, None, :]) * QSCALE).astype(
        jnp.bfloat16
    )
    query_rows = queries.transpose(1, 0, 2).reshape(heads * count, head)
    keys = rotate(key_raw, angles).astype(jnp.bfloat16)
    values = value_raw.astype(jnp.bfloat16)
    all_keys, all_values = side_by_side((keys, values), "ctx", 0, 1)

    def probabilities(top, total):
        scores = jnp.einsum("qd,kd->qk", query_rows, all_keys, preferred_element_type=jnp.float32)
        bent = jnp.tanh(scores / CAP)
        masked = jnp.where(
            allowed[None], (CAP * bent).reshape(heads, count, length), -1e30
        ).reshape(heads * count, length)
        if top is None:
            top = jnp.max(masked, axis=1, keepdims=True)
            expo = jnp.exp(masked - top)
            total = jnp.sum(expo, axis=1, keepdims=True)
        else:
            expo = jnp.exp(masked - top)
        return (expo / total, bent, top, total)

    probs, bent, top, total = probabilities(None, None)
    mixed_rows = product(probs.astype(jnp.bfloat16), all_values)
    attended = (
        mixed_rows.reshape(heads, count, head)
        .transpose(1, 0, 2)
        .reshape(count, heads * head)
        .astype(jnp.bfloat16)
    )
    projected = product(attended, mixing_full)
    second = inputs + rms_scale(projected, mixed_scale)
    middle_in = rms_scale(second, middle_scale).astype(jnp.bfloat16)
    gate_full, up_full, down_full = fetch_columns(gate_weight, up_weight, down_weight)
    middle_rows = lax.all_gather(middle_in, "ctx", axis=0, tiled=True)
    gate = product(middle_rows, gate_full)
    up = product(middle_rows, up_full)
    hidden = gated(gate, up).astype(jnp.bfloat16)
    feed = lax.psum_scatter(
        product(hidden, down_full).astype(jnp.bfloat16), "ctx", scatter_dimension=0, tiled=True
    ).astype(jnp.float32)
    result = second + rms_scale(feed, closing_scale)
    layer_output = result.astype(jnp.bfloat16)
    incoming = cotangent.astype(jnp.float32)
    gate_full, up_full, down_full = fetch_columns(gate_weight, up_weight, down_weight)
    unused, closing_back = jax.vjp(rms_scale, feed, closing_scale)
    feed_grad, closing_term = closing_back(incoming)
    feed_low = feed_grad.astype(jnp.bfloat16)
    feed_rows = lax.all_gather(feed_low, "ctx", axis=0, tiled=True)
    down_term = outer(hidden, feed_rows)
    hidden_back = through(feed_rows, down_full)
    unused, gated_back = jax.vjp(gated, gate, up)
    gate_grad, up_grad = gated_back(hidden_back)
    gate_low = gate_grad.astype(jnp.bfloat16)
    up_low = up_grad.astype(jnp.bfloat16)
    gate_term = outer(middle_rows, gate_low)
    up_term = outer(middle_rows, up_low)
    middle_back = lax.psum_scatter(
        (through(gate_low, gate_full) + through(up_low, up_full)).astype(jnp.bfloat16),
        "ctx",
        scatter_dimension=0,
        tiled=True,
    ).astype(jnp.float32)
    gate_delta, up_delta, down_delta = return_columns(gate_term, up_term, down_term)
    unused, middle_vjp = jax.vjp(rms_scale, second, middle_scale)
    second_part, middle_term = middle_vjp(middle_back)
    second_delta = incoming + second_part
    query_full, key_full, value_full, mixing_full = (
        *side_by_side((query_weight, key_weight, value_weight), ("seq", "ctx"), 0, 1),
        lax.all_gather(mixing_weight, ("seq", "ctx"), axis=0, tiled=True),
    )
    unused, mixed_vjp = jax.vjp(rms_scale, projected, mixed_scale)
    projected_grad, mixed_term = mixed_vjp(second_delta)
    projected_low = projected_grad.astype(jnp.bfloat16)
    mixing_term = outer(attended, projected_low)
    attended_low = through(projected_low, mixing_full).astype(jnp.bfloat16)
    back_rows = (
        attended_low.reshape(count, heads, head).transpose(1, 0, 2).reshape(heads * count, head)
    )
    probs, bent, top, total = probabilities(top, total)
    value_term = outer(probs.astype(jnp.bfloat16), back_rows)
    prob_back = jnp.einsum("qd,kd->qk", back_rows, all_values, preferred_element_type=jnp.float32)
    weighted = jnp.sum(prob_back * probs, axis=1, keepdims=True)
    capped_back = probs * (prob_back - weighted)
    score_low = (capped_back * (1.0 - bent * bent)).astype(jnp.bfloat16)
    query_back = product(score_low, all_keys)
    key_term = outer(score_low, query_rows)
    key_sum, value_sum = tuple(
        (
            part.astype(jnp.float32)
            for part in side_by_side_2(
                (key_term.astype(jnp.bfloat16), value_term.astype(jnp.bfloat16)), "ctx", 0, 1
            )
        )
    )
    query_grad = query_back.reshape(heads, count, head).transpose(1, 0, 2) * QSCALE
    query_low = (
        rotate(query_grad, -angles[:, None, :]).reshape(count, heads * head).astype(jnp.bfloat16)
    )
    key_low = rotate(key_sum, -angles).astype(jnp.bfloat16)
    value_low = value_sum.astype(jnp.bfloat16)
    query_term = outer(entry_in, query_low)
    key_wterm = outer(entry_in, key_low)
    value_wterm = outer(entry_in, value_low)
    entry_back = (
        through(query_low, query_full) + through(key_low, key_full) + through(value_low, value_full)
    )
    unused, entry_vjp = jax.vjp(rms_scale, inputs, entry_scale)
    input_part, entry_term = entry_vjp(entry_back)
    input_delta = second_delta + input_part
    (
        query_delta,
        key_delta,
        value_delta,
        mixing_delta,
        entry_delta,
        mixed_delta,
        middle_delta,
        closing_delta,
    ) = sum_together(
        (
            query_term,
            key_wterm,
            value_wterm,
            mixing_term,
            entry_term,
            mixed_term,
            middle_term,
            closing_term,
        ),
        ("seq", "ctx"),
        (0, 0, 0, 0, 0, 0, 0, 0),
    )
    return (
        layer_output,
        input_delta,
        query_delta,
        key_delta,
        value_delta,
        mixing_delta,
        gate_delta,
        up_delta,
        down_delta,
        entry_delta,
        mixed_delta,
        middle_delta,
        closing_delta,
    )


def solution(mesh):
    in_specs = (
        P(("seq", "ctx"), None),
        P("seq"),
        P(("seq", "ctx"), None),
        P(("seq", "ctx"), None),
        P(("seq", "ctx"), None),
        P(("seq", "ctx"), None),
        P(("seq", "ctx"), None),
        P(("seq", "ctx"), None),
        P(("seq", "ctx"), None),
        P(("seq", "ctx")),
        P(("seq", "ctx")),
        P(("seq", "ctx")),
        P(("seq", "ctx")),
        P(("seq", "ctx"), None),
    )
    out_specs = (
        P(("seq", "ctx"), None),
        P(("seq", "ctx"), None),
        P(("seq", "ctx"), None),
        P(("seq", "ctx"), None),
        P(("seq", "ctx"), None),
        P(("seq", "ctx"), None),
        P(("seq", "ctx"), None),
        P(("seq", "ctx"), None),
        P(("seq", "ctx"), None),
        P(("seq", "ctx")),
        P(("seq", "ctx")),
        P(("seq", "ctx")),
        P(("seq", "ctx")),
    )
    return jax.shard_map(body, mesh=mesh, in_specs=in_specs, out_specs=out_specs, check_vma=False)
```

profile of v0, /device:TPU:1, one launch (start us, length us, event | category | flops | bytes accessed | tf_op | source)
XLA Modules:
  0.0 1188.0 jit_solution(9386453286972627734)
XLA Ops:
  12.1 69.1 %all-reduce.8 = (bf16[1152]{0:T(1024)(128)(2,1)S(1)}, bf16[1152]{0:T(1024)(128)(2,1)S(1)}, bf16[1152]{0:T(1024)(128)(2,1)S(1)}, bf16[1152]{0:T(1024)(128)(2,1)S(1)}) all-reduce(bf16[1152]{0:T(1024)(128)(2,1)S(1)} %dynamic-update-slice, bf16[1152]{0:T(1024)(128)(2,1)S(1)} %dynamic-update-slice.1, ...), channel_id=1, replica_groups=mesh['seq'=8,'ctx'=16] {'seq','ctx'}, use_global_device_ids=true, to_apply=%add.1 | all-reduce | flops 4608 | bytes 18432
  82.4 132.1 %all-gather.19.cloned.1.call-done = bf16[128,9,1536]{2,1,0:T(8,128)(2,1)} async-done(((bf16[1,9,1536]{2,1,0:T(8,128)(2,1)}), bf16[128,9,1536]{2,1,0:T(8,128)(2,1)}) %all-gather.19.cloned.1.call-update) | async-done | bytes 3538960 | tf_op jit(solution)/shard_map/all_gather | solution.py:29
  214.5 7.5 reshape.419
  229.5 15.4 %all_to_all.41 = bf16[16,2,3888]{2,1,0:T(2,128)(2,1)S(1)} all-to-all(bf16[16,2,3888]{2,1,0:T(2,128)(2,1)S(1)} %reshape.430), channel_id=1, replica_groups=mesh['seq'=8,'ctx'=16] {'ctx'}, dimensions={0} | all-to-all | bytes 497664 | tf_op jit(solution)/shard_map/all_to_all | solution.py:20
  250.8 23.8 %all-gather.9.cloned.1.call-done = bf16[2048,512]{1,0:T(8,128)(2,1)} async-done(((bf16[128,512]{1,0:T(8,128)(2,1)}), bf16[2048,512]{1,0:T(8,128)(2,1)}) %all-gather.9.cloned.1.call-update) | async-done | bytes 2097168 | tf_op jit(solution)/shard_map/all_gather | solution.py:29
  283.5 187.1 %all-gather.11.cloned.1.call-done = bf16[1024,1152]{1,0:T(8,128)(2,1)} async-done(((bf16[8,1152]{1,0:T(8,128)(2,1)}), bf16[1024,1152]{1,0:T(8,128)(2,1)}) %all-gather.11.cloned.1.call-update) | async-done | bytes 2359312 | tf_op jit(solution)/shard_map/all_gather | solution.py:183
  474.3 29.7 %all-gather.1 = bf16[8,54,1152]{2,1,0:T(8,128)(2,1)S(1)} all-gather(bf16[1,54,1152]{2,1,0:T(8,128)(2,1)S(1)} %bitcast.133), channel_id=1, replica_groups=mesh['seq'=8,'ctx'=16] {'seq'}, dimensions={0}, use_global_device_ids=true | all-gather | bytes 1119744 | tf_op jit(solution)/shard_map/all_gather | solution.py:107
  505.3 31.1 %all-gather.15.cloned.1.call-done = bf16[1152,16,1,54]{3,1,2,0:T(8,128)(2,1)} async-done(((bf16[144,16,1,54]{3,1,2,0:T(8,128)(2,1)}), bf16[1152,16,1,54]{3,1,2,0:T(8,128)(2,1)}) %all-gather.15.cloned.1.call-update) | async-done | bytes 1990672 | tf_op jit(solution)/shard_map/all_gather | solution.py:29
  546.9 48.9 %all-gather.13.cloned.1.call-done = bf16[2048,1152]{1,0:T(8,128)(2,1)} async-done(((bf16[128,1152]{1,0:T(8,128)(2,1)}), bf16[2048,1152]{1,0:T(8,128)(2,1)}) %all-gather.13.cloned.1.call-update) | async-done | bytes 4718608 | tf_op jit(solution)/shard_map/all_gather | solution.py:231
  612.3 80.1 %reduce-scatter.9.cloned.1.call-done = bf16[128,1152]{1,0:T(8,128)(2,1)} async-done(((bf16[2048,1152]{1,0:T(8,128)(2,1)}), bf16[128,1152]{1,0:T(8,128)(2,1)}) %reduce-scatter.9.cloned.1.call-update) | async-done | bytes 294928 | tf_op jit(solution)/shard_map/reduce_scatter | solution.py:235
  696.9 58.2 %all-gather.17.cloned.1.call-done = bf16[2048,1152]{1,0:T(8,128)(2,1)} async-done(((bf16[128,1152]{1,0:T(8,128)(2,1)}), bf16[2048,1152]{1,0:T(8,128)(2,1)}) %all-gather.17.cloned.1.call-update) | async-done | bytes 4718608 | tf_op jit(solution)/shard_map/all_gather | solution.py:245
  755.2 9.3 multiply_convert_fusion.1
  772.5 79.9 %reduce-scatter.11.cloned.1.call-done = bf16[128,1152]{1,0:T(8,128)(2,1)} async-done(((bf16[2048,1152]{1,0:T(8,128)(2,1)}), bf16[128,1152]{1,0:T(8,128)(2,1)}) %reduce-scatter.11.cloned.1.call-update) | async-done | bytes 294928 | tf_op jit(solution)/shard_map/reduce_scatter | solution.py:254
  885.1 5.8 copy.81
  890.9 8.1 reshape.425
  913.2 26.7 %reduce-scatter.13.cloned.1.call-done = bf16[128,512]{1,0:T(8,128)(2,1)} async-done(((bf16[2048,512]{1,0:T(8,128)(2,1)}), bf16[128,512]{1,0:T(8,128)(2,1)}) %reduce-scatter.13.cloned.1.call-update) | async-done | bytes 131088 | tf_op jit(solution)/shard_map/reduce_scatter | solution.py:39
  946.7 6.1 reshape_reshape.12
  962.3 13.0 %concatenate.44 = f32[128,23076]{1,0:T(8,128)} concatenate(f32[128,9216]{1,0:T(8,128)} %reshape_reshape.12, f32[128,2304]{1,0:T(8,128)S(1)} %reshape_reshape.13, f32[128,2304]{1,0:T(8,128)S(1)} %reshape_reshape.14, f32[128,9216]{1,0:T(8,128)} %reshape_reshape.15, f32[128,9]{1,0:T(8,128)} %reshape.392, f32[128,9]{1,0:T(8,128)S(1)} %reshape.393, f32[128,9]{1,0:T(8,128)} %reshape.394, ...), dimensions={1} | concatenate | bytes 23629824 | tf_op jit(solution)/shard_map/concatenate | solution.py:51
  975.2 10.0 pad.4
  985.3 11.5 reshape.396
  1002.1 27.0 %fusion = bf16[64,1152]{1,0:T(8,128)(2,1)S(1)} fusion(bf16[432,1152]{1,0:T(8,128)(2,1)S(1)} %convolution_convert_fusion.3), kind=kCustom, calls=%all-reduce-scatter | all-reduce-scatter fusion | flops 589825 | bytes 1143296
  1039.9 11.4 all-to-all-start.1
  1052.0 7.9 all-to-all-done.1
  1064.4 111.2 %all-reduce.11.cloned.1.call-done = f32[23552,128]{1,0:T(8,128)} async-done(((f32[23552,128]{1,0:T(8,128)}), f32[23552,128]{1,0:T(8,128)}) %all-reduce.11.cloned.1.call-update) | async-done | bytes 12058640
  (248 shorter events, 161.0 us)
Async XLA Ops:
  7.2 207.3 %all-gather.19.cloned.1.call-start = ((), (), s32[]{:S(2)}) async-start(), calls=%async_computation.14 | async-start | bytes 6340608 | tf_op jit(solution)/shard_map/all_gather | solution.py:29
  8.7 265.9 %all-gather.9.cloned.1.call-start = ((), (), s32[]{:S(2)}) async-start(), calls=%async_computation.6 | async-start | bytes 2228224 | tf_op jit(solution)/shard_map/all_gather | solution.py:29
  81.2 143.5 %copy-start.35 = (f32[128]{0:T(128)}, f32[128]{0:T(128)S(1)}, u32[]{:S(2)}) copy-start(f32[128]{0:T(128)S(1)} %negate_power_fusion) | copy-start | bytes 1540
  81.3 143.5 %copy-start.37 = (f32[128]{0:T(128)}, f32[128]{0:T(128)S(1)}, u32[]{:S(2)}) copy-start(f32[128]{0:T(128)S(1)} %fusion.62) | copy-start | bytes 1540
  82.4 139.6 %copy-start.40 = (f32[128]{0:T(128)}, f32[128]{0:T(128)S(1)}, u32[]{:S(2)}) copy-start(f32[128]{0:T(128)S(1)} %fusion.42) | copy-start | bytes 1540
  82.4 165.7 %copy-start.30 = (f32[128]{0:T(128)}, f32[128]{0:T(128)S(1)}, u32[]{:S(2)}) copy-start(f32[128]{0:T(128)S(1)} %fusion.56) | copy-start | bytes 1540
  82.4 139.6 %copy-start.2 = (bf16[128,1152]{1,0:T(8,128)(2,1)S(1)}, bf16[128,1152]{1,0:T(8,128)(2,1)}, u32[]{:S(2)}) copy-start(bf16[128,1152]{1,0:T(8,128)(2,1)} %param.14) | copy-start | bytes 884740
  82.4 144.2 %copy-start.25 = (bf16[9,6912]{1,0:T(8,128)(2,1)S(1)}, bf16[9,6912]{1,0:T(8,128)(2,1)}, u32[]{:S(2)}) copy-start(bf16[9,6912]{1,0:T(8,128)(2,1)} %param.20) | copy-start | bytes 373252
  225.8 244.8 %all-gather.11.cloned.1.call-start = ((), (), s32[]{:S(2)}) async-start(), calls=%async_computation.7 | async-start | bytes 2377728 | tf_op jit(solution)/shard_map/all_gather | solution.py:183
  226.5 309.8 %all-gather.15.cloned.1.call-start = ((), (), s32[]{:S(2)}) async-start(), calls=%async_computation.9 | async-start | bytes 5308416 | tf_op jit(solution)/shard_map/all_gather | solution.py:29
  246.6 349.2 %all-gather.13.cloned.1.call-start = ((), (), s32[]{:S(2)}) async-start(), calls=%async_computation.8 | async-start | bytes 5013504 | tf_op jit(solution)/shard_map/all_gather | solution.py:231
  283.3 191.0 %copy-start.27 = (bf16[54,1152]{1,0:T(8,128)(2,1)S(1)}, bf16[54,1152]{1,0:T(8,128)(2,1)}, u32[]{:S(2)}) copy-start(bf16[54,1152]{1,0:T(8,128)(2,1)} %param.22) | copy-start | bytes 373252
  283.5 190.8 %copy-start.11 = (bf16[128,4,256]{0,2,1:T(8,128)(2,1)}, bf16[128,4,256]{0,2,1:T(8,128)(2,1)S(1)}, u32[]{:S(2)}) copy-start(bf16[128,4,256]{0,2,1:T(8,128)(2,1)S(1)} %copy.62) | copy-start | bytes 786436
  474.3 218.1 %reduce-scatter.9.cloned.1.call-start = ((), (), s32[]{:S(2)}) async-start(), calls=%async_computation.10 | async-start | bytes 5013504 | tf_op jit(solution)/shard_map/reduce_scatter | solution.py:235
  612.2 81.3 %copy-start.10 = (bf16[128,1152]{1,0:T(8,128)(2,1)S(1)}, bf16[128,1152]{1,0:T(8,128)(2,1)}, u32[]{:S(2)}) copy-start(bf16[128,1152]{1,0:T(8,128)(2,1)} %param.27) | copy-start | bytes 884740
  612.3 142.9 %all-gather.17.cloned.1.call-start = ((), (), s32[]{:S(2)}) async-start(), calls=%async_computation.11 | async-start | bytes 5013504 | tf_op jit(solution)/shard_map/all_gather | solution.py:245
  696.6 155.8 %reduce-scatter.11.cloned.1.call-start = ((), (), s32[]{:S(2)}) async-start(), calls=%async_computation.12 | async-start | bytes 5013504 | tf_op jit(solution)/shard_map/reduce_scatter | solution.py:254
  772.2 87.6 %copy-start.3 = (bf16[1024,1152]{1,0:T(8,128)(2,1)S(1)}, bf16[1024,1152]{1,0:T(8,128)(2,1)}, u32[]{:S(2)}) copy-start(bf16[1024,1152]{1,0:T(8,128)(2,1)} %all-gather.11.cloned.1.call-done) | copy-start | bytes 7077892
  772.2 167.7 %reduce-scatter.13.cloned.1.call-start = ((), (), s32[]{:S(2)}) async-start(), calls=%async_computation.13 | async-start | bytes 2228224 | tf_op jit(solution)/shard_map/reduce_scatter | solution.py:39
  870.9 165.3 %reduce-scatter.15.cloned.1.call-start = ((), (), s32[]{:S(2)}) async-start(), calls=%async_computation.15 | async-start | bytes 2322432
  899.1 276.6 %all-reduce.11.cloned.1.call-start = ((), (), s32[]{:S(2)}) async-start(), calls=%async_computation.16 | async-start | bytes 24117248
  1029.1 6.3 collective-permute-start
  1031.3 4.1 collective-permute-start.1
  1039.9 20.0 %all-to-all-start.1 = ((bf16[16,2,3888]{2,1,0:T(2,128)(2,1)}), bf16[16,2,3888]{2,1,0:T(2,128)(2,1)S(1)}, u32[]{:S(2)}, u32[]{:S(2)}) async-start(bf16[16,2,3888]{2,1,0:T(2,128)(2,1)} %reshape.432), calls=%async_computation.4 | async-start | bytes 507904 | tf_op jit(solution)/shard_map/all_to_all | solution.py:20
  (39 other events, 644.8 us)
Sparse Core Ops, SparseCore 0:
  10.3 204.1 all-gather.18
  225.9 48.6 all-gather.8
  276.3 194.1 all-gather.10
  472.1 64.2 all-gather.14
  539.2 56.4 all-gather.12
  612.4 79.9 reduce-scatter.8
  696.8 58.3 all-gather.16
  772.3 80.0 reduce-scatter.10
  871.0 68.9 reduce-scatter.12
  942.2 38.7 reduce-scatter.14
  996.9 178.7 all-reduce.10
where the time goes:
time: 1200 us; the launch traced here: 1190 us
  waiting for transfers between devices  788 us (66%)
  blocking collectives  141 us (12%)
  local copies, waits for them, and re-layouts  114 us (10%)
  matrix products  79.6 us (7%)
  other arithmetic  30.3 us (3%)
  starting transfers between devices  18.6 us (2%)
  between operations  16.4 us (1%)
    all_gather x1, waiting for transfers between devices, body(): lax.all_gather(mixing_weight, ('seq', 'ctx'), axis=0, tiled=True)  187 us
    all_gather x3, waiting for transfers between devices, side_by_side(): lax.all_gather(both, axis, axis=dim, tiled=True)  187 us
    unnamed x15, waiting for transfers between devices  112 us
    unnamed x2, blocking collectives  96.1 us
    reduce_scatter x1, waiting for transfers between devices, body(): lax.psum_scatter(product(hidden, down_full).astype(jnp.bfloat16), 'ctx',...  80.1 us
    reduce_scatter x1, waiting for transfers between devices, body(): lax.psum_scatter((through(gate_low, gate_full) + through(up_low, up_full)...  79.9 us
    all_gather x1, waiting for transfers between devices, body(): feed_rows = lax.all_gather(feed_low, 'ctx', axis=0, tiled=True)  58.2 us
    all_gather x1, waiting for transfers between devices, body(): middle_rows = lax.all_gather(middle_in, 'ctx', axis=0, tiled=True)  48.9 us
  transfers between devices with their start and end apart: 14, of which 11 were waited for; matrix products, arithmetic and copies ran while one was open for 15% of the time, Pallas kernels for 0%

commit v1 on v0

v1 whole, which is shorter than its diff:
```python
import jax
import jax.numpy as jnp
from jax import lax
from jax.sharding import Mesh
from jax.sharding import PartitionSpec as P

EPS = 1e-06
CAP = 20.0
QSCALE = 0.0625
THETA = 1000000.0

AXES = ("yl", "z", "yh", "x", "c")
SIZES = (2, 4, 2, 4, 2)
PLANE = ("z", "yh", "yl")
RING = ("x", "c")


def moved(step):
    pairs = []
    for yl in range(2):
        for z in range(4):
            for yh in range(2):
                for x in range(4):
                    for c in range(2):
                        to = step(yh * 2 + yl, z, x, c)
                        y2, z2, x2, c2 = (to[0] % 4, to[1] % 4, to[2] % 4, to[3] % 2)
                        here = (((yl * 4 + z) * 2 + yh) * 4 + x) * 2 + c
                        there = (((y2 % 2 * 4 + z2) * 2 + y2 // 2) * 4 + x2) * 2 + c2
                        pairs.append((here, there))
    return pairs


HOPS = {
    "c": moved(lambda y, z, x, c: (y, z, x, c + 1)),
    "y2": moved(lambda y, z, x, c: (y + 2, z, x, c)),
}
for n in (1, 2, 3):
    HOPS["x", n] = moved(lambda y, z, x, c: (y, z, x + n, c))
    HOPS["y", n] = moved(lambda y, z, x, c: (y + n, z, x, c))
    HOPS["z", n] = moved(lambda y, z, x, c: (y, z + n, x, c))


def hop(values, way):
    return lax.ppermute(values, AXES, HOPS[way])


def rms_scale(values, gain):
    return values * lax.rsqrt(jnp.mean(values * values, axis=-1, keepdims=True) + EPS) * gain


def rotate(values, angles):
    half = values.shape[-1] // 2
    first = values[..., :half]
    second = values[..., half:]
    cosine = jnp.cos(angles)
    sine = jnp.sin(angles)
    return jnp.concatenate(
        [first * cosine - second * sine, second * cosine + first * sine], axis=-1
    )


def outer(left, right):
    return lax.dot_general(
        left, right, (((0,), (0,)), ((), ())), preferred_element_type=jnp.float32
    )


def through(left, weight):
    return lax.dot_general(
        left, weight, (((1,), (1,)), ((), ())), preferred_element_type=jnp.float32
    )


def product(left, right):
    return jnp.dot(left, right, preferred_element_type=jnp.float32)


def low(values):
    return values.astype(jnp.bfloat16)


def gated(gate, up):
    return jax.nn.gelu(gate, approximate=True) * up


def ring_rows(rows):
    near = jnp.concatenate([rows, hop(rows, ("x", 1)), hop(rows, ("x", 3)), hop(rows, ("x", 2))])
    return near, hop(near, "c")


def ring_sums(near, far):
    count = near.shape[0] // 4
    both = low(near.astype(jnp.float32) + hop(far, "c").astype(jnp.float32))
    own, back, ahead, across = (both[k * count : (k + 1) * count] for k in range(4))
    parts = (hop(back, ("x", 3)), hop(ahead, ("x", 1)), hop(across, ("x", 2)))
    total = own.astype(jnp.float32)
    for part in parts:
        total = total + part.astype(jnp.float32)
    return total


def gather_all(rows):
    for axis in ("z", "y", "x"):
        rows = jnp.concatenate([rows, *(hop(rows, (axis, n)) for n in (3, 2, 1))])
    return jnp.concatenate([rows, hop(rows, "c")])


def scatter_all(term):
    half = term.shape[0] // 2
    term = term[:half].astype(jnp.float32) + hop(term[half:], "c").astype(jnp.float32)
    for axis in ("x", "y", "z"):
        term = low(term)
        cut = term.shape[0] // 4
        parts = [hop(term[n * cut : (n + 1) * cut], (axis, n)) for n in (1, 2, 3)]
        term = term[:cut].astype(jnp.float32)
        for part in parts:
            term = term + part.astype(jnp.float32)
    return term


def by_distance(size):
    here = {axis: lax.axis_index(axis) for axis in AXES}
    block = size // 128
    place = jnp.arange(size, dtype=jnp.int32)
    r, q = (place % block, place // block)
    z = (here["z"] + q) % 4
    y = (here["yh"] * 2 + here["yl"] + q // 4) % 4
    x = (here["x"] + q // 16) % 4
    c = (here["c"] + q // 64) % 2
    source = ((((y % 2 * 4 + z) * 2 + y // 2) * 4 + x) * 2 + c) * block + r
    return low(jnp.arange(size, dtype=jnp.int32)[:, None] == source[None, :])


def body(
    tokens,
    prefix_len,
    query_weight,
    key_weight,
    value_weight,
    mixing_weight,
    gate_weight,
    up_weight,
    down_weight,
    entry_gain,
    mixed_gain,
    middle_gain,
    closing_gain,
    cotangent,
):
    count, width = tokens.shape
    head = key_weight.shape[1]
    heads = query_weight.shape[1] // head
    half = head // 2
    own = gate_weight.shape[0]
    units = down_weight.shape[0]
    units_pad = -(-units // 8) * 8
    hidden_units = 16 * units_pad
    wide = 2 * hidden_units
    own_mix = mixing_weight.shape[0]
    x, c, yh = (lax.axis_index("x"), lax.axis_index("c"), lax.axis_index("yh"))

    def columns(weight):
        cut = weight.reshape(own, 2, 4, 2, 8, units)
        cut = jnp.pad(cut, ((0, 0),) * 5 + ((0, units_pad - units),))
        return cut.transpose(4, 0, 2, 3, 1, 5).reshape(8, own, hidden_units)

    gate_up = jnp.concatenate([columns(gate_weight), columns(up_weight)], axis=2)
    mixing_own = jnp.pad(mixing_weight, ((0, 0), (0, wide - width)))
    mixing_own = jnp.broadcast_to(mixing_own, (8, own_mix, wide))
    ring = lax.all_to_all(
        jnp.concatenate([gate_up, mixing_own], axis=1), RING, 0, 0, tiled=True
    )
    down_own = jnp.pad(down_weight, ((0, units_pad - units), (0, wide - width)))
    plane = lax.all_gather(
        jnp.concatenate(
            [
                ring[:, :own].reshape(8 * own, wide),
                down_own,
                ring[:, own:].reshape(8 * own_mix, wide),
            ]
        ),
        PLANE,
        axis=0,
    )
    ends = (8 * own, 8 * own + units_pad)
    gate_up_full = (
        plane[:, : ends[0]].reshape(4, 2, 2, ends[0], wide).transpose(2, 0, 1, 3, 4)
    ).reshape(width, wide)
    down_full = plane[:, ends[0] : ends[1], :width].reshape(hidden_units, width)
    mixing_full = (
        plane[:, ends[1] :, :width].reshape(4, 2, 2, 8 * own_mix, width).transpose(2, 0, 1, 3, 4)
    ).reshape(heads * head, width)

    qkv_own = jnp.concatenate([query_weight, key_weight, value_weight], axis=1)
    gains_own = jnp.stack([entry_gain, mixed_gain, middle_gain, closing_gain], axis=1)
    gathered = gather_all(
        jnp.concatenate([qkv_own, jnp.pad(gains_own, ((0, 0), (0, 124)))], axis=1)
    )
    qkv_full = gathered[:, : qkv_own.shape[1]]
    entry_order = by_distance(width)
    gains = lax.dot_general(
        gathered[:, qkv_own.shape[1] :],
        entry_order,
        (((0,), (1,)), ((), ())),
        preferred_element_type=jnp.float32,
    )
    entry_scale, mixed_scale, middle_scale, closing_scale = (gains[k] for k in range(4))

    def positions(xs, ys, cs):
        place = ((yh ^ ys) * 4 + (x + xs) % 4) * 2 + (c ^ cs)
        return place * count + jnp.arange(count, dtype=jnp.int32)

    query_pos = positions(0, 0, 0)
    key_pos = jnp.concatenate(
        [positions(xs, ys, cs) for cs in (0, 1) for xs in (0, 3, 1, 2) for ys in (0, 1)]
    )
    length = key_pos.shape[0]
    allowed = (key_pos[None, :] <= query_pos[:, None]) | (key_pos[None, :] < prefix_len[0])
    inverse = 1.0 / THETA ** (jnp.arange(half, dtype=jnp.float32) * (2.0 / head))
    angles = query_pos.astype(jnp.float32)[:, None] * inverse[None, :]
    inputs = tokens.astype(jnp.float32)

    entry_in = low(rms_scale(inputs, entry_scale))
    entry_near = low(product(entry_in, entry_order))
    qkv = product(entry_near, qkv_full)
    query_raw, key_raw, value_raw = jnp.split(qkv, [heads * head, (heads + 1) * head], axis=1)
    queries = low(rotate(query_raw.reshape(count, heads, head), angles[:, None, :]) * QSCALE)
    query_rows = queries.transpose(1, 0, 2).reshape(heads * count, head)
    pairs = jnp.concatenate([low(rotate(key_raw, angles)), low(value_raw)], axis=1)
    near, far = ring_rows(jnp.concatenate([pairs, hop(pairs, "y2")]))
    pairs = jnp.concatenate([near, far])
    all_keys, all_values = (pairs[:, :head], pairs[:, head:])

    def probabilities(top, total):
        scores = through(query_rows, all_keys)
        bent = jnp.tanh(scores / CAP)
        masked = jnp.where(
            allowed[None], (CAP * bent).reshape(heads, count, length), -1e30
        ).reshape(heads * count, length)
        if top is None:
            top = jnp.max(masked, axis=1, keepdims=True)
            expo = jnp.exp(masked - top)
            total = jnp.sum(expo, axis=1, keepdims=True)
        else:
            expo = jnp.exp(masked - top)
        return (expo / total, bent, top, total)

    probs, bent, top, total = probabilities(None, None)
    mixed_rows = product(low(probs), all_values)
    attended = low(
        mixed_rows.reshape(heads, count, head).transpose(1, 0, 2).reshape(count, heads * head)
    )
    projected = product(attended, mixing_full)
    second = inputs + rms_scale(projected, mixed_scale)
    middle_in = low(rms_scale(second, middle_scale))

    middle_parts = ring_rows(middle_in)
    gates, ups, hiddens = ([], [], [])
    for rows in middle_parts:
        both = product(rows, gate_up_full)
        gates.append(both[:, :hidden_units])
        ups.append(both[:, hidden_units:])
        hiddens.append(low(gated(gates[-1], ups[-1])))
    feed = ring_sums(*(low(product(hidden, down_full)) for hidden in hiddens))
    layer_output = low(second + rms_scale(feed, closing_scale))

    incoming = cotangent.astype(jnp.float32)
    unused, closing_back = jax.vjp(rms_scale, feed, closing_scale)
    feed_grad, closing_term = closing_back(incoming)
    feed_parts = ring_rows(low(feed_grad))
    lows = []
    for rows, gate, up in zip(feed_parts, gates, ups):
        unused, gated_back = jax.vjp(gated, gate, up)
        gate_grad, up_grad = gated_back(through(rows, down_full))
        lows.append(jnp.concatenate([low(gate_grad), low(up_grad)], axis=1))
    middle_back = ring_sums(*(low(through(rows, gate_up_full)) for rows in lows))
    gate_up_term = low(outer(jnp.concatenate(middle_parts), jnp.concatenate(lows)))
    down_term = low(outer(jnp.concatenate(hiddens), jnp.concatenate(feed_parts)))
    gate_up_term = gate_up_term.reshape(2, 4, 2, 8 * own, wide).transpose(1, 2, 0, 3, 4)
    down_term = jnp.pad(
        down_term.reshape(16, units_pad, width), ((0, 0), (0, 0), (0, wide - width))
    )
    plane_term = jnp.concatenate([gate_up_term.reshape(16, 8 * own, wide), down_term], axis=1)
    plane_sum = lax.psum_scatter(
        plane_term.reshape(-1, wide), PLANE, scatter_dimension=0, tiled=True
    )
    down_delta = plane_sum[8 * own : 8 * own + units, :width].astype(jnp.float32)
    gate_up_sum = lax.all_to_all(
        plane_sum[: 8 * own].reshape(8, own, wide), RING, 0, 0, tiled=True
    )
    gate_up_sum = gate_up_sum.astype(jnp.float32).reshape(8, own, 2, 4, 2, 2, units_pad)
    gate_up_sum = gate_up_sum[..., :units].transpose(2, 1, 5, 3, 4, 0, 6).reshape(2, own, -1)
    gate_delta, up_delta = (gate_up_sum[0], gate_up_sum[1])

    unused, middle_vjp = jax.vjp(rms_scale, second, middle_scale)
    second_part, middle_term = middle_vjp(middle_back)
    second_delta = incoming + second_part
    unused, mixed_vjp = jax.vjp(rms_scale, projected, mixed_scale)
    projected_grad, mixed_term = mixed_vjp(second_delta)
    projected_low = low(projected_grad)
    attended_low = low(through(projected_low, mixing_full))
    attended_near = low(product(attended, by_distance(heads * head)))
    mixing_term = low(outer(attended_near, projected_low))
    mixing_delta = scatter_all(mixing_term)
    back_rows = (
        attended_low.reshape(count, heads, head).transpose(1, 0, 2).reshape(heads * count, head)
    )
    probs, bent, top, total = probabilities(top, total)
    value_term = outer(low(probs), back_rows)
    prob_back = through(back_rows, all_values)
    weighted = jnp.sum(prob_back * probs, axis=1, keepdims=True)
    capped_back = probs * (prob_back - weighted)
    score_low = low(capped_back * (1.0 - bent * bent))
    query_back = product(score_low, all_keys)
    key_term = outer(score_low, query_rows)
    pair_term = low(jnp.concatenate([key_term, value_term], axis=1))
    pair_sum = ring_sums(pair_term[: length // 2], pair_term[length // 2 :])
    pair_sum = pair_sum[:count] + hop(low(pair_sum[count:]), "y2").astype(jnp.float32)
    query_grad = query_back.reshape(heads, count, head).transpose(1, 0, 2) * QSCALE
    query_low = rotate(query_grad, -angles[:, None, :]).reshape(count, heads * head)
    key_low = rotate(pair_sum[:, :head], -angles)
    qkv_low = low(jnp.concatenate([query_low, key_low, pair_sum[:, head:]], axis=1))
    back_near = through(qkv_low, qkv_full)
    back_high = low(back_near)
    back_rest = low(back_near - back_high.astype(jnp.float32))
    entry_back = through(back_high, entry_order) + through(back_rest, entry_order)
    unused, entry_vjp = jax.vjp(rms_scale, inputs, entry_scale)
    input_part, entry_term = entry_vjp(entry_back)
    input_delta = second_delta + input_part

    qkv_term = outer(entry_near, qkv_low)
    gain_terms = jnp.stack([entry_term, mixed_term, middle_term, closing_term])
    gain_terms = jnp.pad(low(gain_terms), ((0, 124), (0, 0)))
    gain_rows = lax.dot_general(
        entry_order, gain_terms, (((0,), (1,)), ((), ())), preferred_element_type=jnp.float32
    )
    qkv_sum = scatter_all(low(jnp.concatenate([qkv_term, gain_rows], axis=1)))
    cuts = [heads * head, (heads + 1) * head, (heads + 2) * head]
    query_delta, key_delta, value_delta, gain_deltas = jnp.split(qkv_sum, cuts, axis=1)
    entry_delta, mixed_delta, middle_delta, closing_delta = (gain_deltas[:, k] for k in range(4))
    return (
        layer_output,
        input_delta,
        query_delta,
        key_delta,
        value_delta,
        mixing_delta,
        gate_delta,
        up_delta,
        down_delta,
        entry_delta,
        mixed_delta,
        middle_delta,
        closing_delta,
    )


def solution(mesh):
    cut = Mesh(mesh.devices.reshape(SIZES), AXES)
    rows = P(AXES, None)
    flat = P(AXES)
    in_specs = (rows, P(("yl", "z")), *(rows,) * 7, *(flat,) * 4, rows)
    out_specs = (*(rows,) * 9, *(flat,) * 4)
    return jax.shard_map(body, mesh=cut, in_specs=in_specs, out_specs=out_specs, check_vma=False)
```

time: 1200 us -> 440 us (0.37)
  waiting for transfers between devices: 788 us -> 168 us
  blocking collectives: 141 us -> 16.8 us
  starting transfers between devices: 18.6 us -> 70.5 us
  local copies, waits for them, and re-layouts: 114 us -> 72.5 us
  matrix products: 79.6 us -> 50 us
    all_gather x6 -> x1, waiting for transfers between devices: 481 us -> 0.02 us  [body(): lax.all_gather(jnp.concatenate([ring[:, :own].reshape(8 * own, wide), dow...]
    reduce_scatter x3 -> x1, waiting for transfers between devices: 187 us -> 0.01 us  [body(): lax.psum_scatter(plane_term.reshape(-1, wide), PLANE, scatter_dimension=0...]
    ppermute x0 -> x56, waiting for transfers between devices: none -> 161 us  [hop(): return lax.ppermute(values, AXES, HOPS[way])]
    unnamed x15 -> x2, waiting for transfers between devices: 112 us -> 0.03 us
    unnamed x2 -> x0, blocking collectives: 96.1 us -> none
    ppermute x0 -> x56, starting transfers between devices: none -> 62 us  [hop(): return lax.ppermute(values, AXES, HOPS[way])]
    all_gather x1 -> x0, blocking collectives: 29.7 us -> none  [fetch_columns(): lax.all_gather(down_weight, 'seq', axis=0, tiled=True)]
    unnamed x119 -> x160, local copies, waits for them, and re-layouts: 39.5 us -> 11.9 us
  transfers between devices with their start and end apart: 14 -> 59, of which waited for: 11 -> 38; matrix products, arithmetic and copies ran while one was open for 15% -> 27% of each run, Pallas kernels for 0% -> 0%
where the time goes in v1:
time: 440 us; the launch traced here: 432 us
  waiting for transfers between devices  168 us (38%)
  local copies, waits for them, and re-layouts  72.5 us (16%)
  starting transfers between devices  70.5 us (16%)
  matrix products  50 us (11%)
  other arithmetic  37.2 us (8%)
  blocking collectives  16.8 us (4%)
  between operations  16.7 us (4%)
    ppermute x56, waiting for transfers between devices, hop(): return lax.ppermute(values, AXES, HOPS[way])  161 us
    ppermute x56, starting transfers between devices, hop(): return lax.ppermute(values, AXES, HOPS[way])  62 us
    dot_general x10, matrix products, through(): lax.dot_general(left, weight, (((1,), (1,)), ((), ())), preferred_element...  21.3 us
    concatenate x1, local copies, waits for them, and re-layouts, gather_all(): return jnp.concatenate([rows, hop(rows, 'c')])  20.9 us
    all_to_all x1, blocking collectives, body(): lax.all_to_all(jnp.concatenate([gate_up, mixing_own], axis=1), RING, 0, 0...  16.8 us
    concatenate x2, local copies, waits for them, and re-layouts, gather_all(): rows = jnp.concatenate([rows, *(hop(rows, (axis, n)) for n in (3, 2, 1))])  14.7 us
    dot_general x9, matrix products, product(): return jnp.dot(left, right, preferred_element_type=jnp.float32)  12.8 us
    dot_general x6, matrix products, outer(): lax.dot_general(left, right, (((0,), (0,)), ((), ())), preferred_element_...  12.7 us
  transfers between devices with their start and end apart: 59, of which 38 were waited for; matrix products, arithmetic and copies ran while one was open for 27% of the time, Pallas kernels for 0%

profile of v1, /device:TPU:1, one launch (start us, length us, event | category | flops | bytes accessed | tf_op | source)
XLA Modules:
  0.0 432.2 jit_solution(3189456103627390933)
XLA Ops:
  11.9 16.8 %all_to_all.10 = bf16[8,17,1792]{2,1,0:T(8,128)(2,1)S(1)} all-to-all(bf16[8,17,1792]{2,1,0:T(8,128)(2,1)S(1)} %copy.81), channel_id=1, replica_groups=mesh['yl'=2,'z'=4,'yh'=2,'x'=4,'c'=2] {'x','c'}, dimensions={0} | all-to-all | bytes 974848 | tf_op jit(solution)/shard_map/all_to_all | solution.py:170
  43.9 5.8 %collective-permute-done.4 = bf16[36,1664]{1,0:T(8,128)(2,1)S(1)} collective-permute-done((bf16[36,1664]{1,0:T(8,128)(2,1)S(1)}, bf16[36,1664]{1,0:T(8,128)(2,1)S(1)}, u32[]{:S(2)}, u32[]{:S(2)}) %collective-permute-start.4) | collective-permute-done | bytes 119840 | tf_op jit(solution)/shard_map/ppermute | solution.py:44
  57.0 11.7 %collective-permute-done.8 = bf16[144,1664]{1,0:T(8,128)(2,1)S(1)} collective-permute-done((bf16[144,1664]{1,0:T(8,128)(2,1)S(1)}, bf16[144,1664]{1,0:T(8,128)(2,1)S(1)}, u32[]{:S(2)}, u32[]{:S(2)}) %collective-permute-start.8) | collective-permute-done | bytes 479264 | tf_op jit(solution)/shard_map/ppermute | solution.py:44
  69.4 7.2 %collective-permute-done.6 = bf16[144,1664]{1,0:T(8,128)(2,1)S(1)} collective-permute-done((bf16[144,1664]{1,0:T(8,128)(2,1)S(1)}, bf16[144,1664]{1,0:T(8,128)(2,1)S(1)}, u32[]{:S(2)}, u32[]{:S(2)}) %collective-permute-start.6) | collective-permute-done | bytes 479264 | tf_op jit(solution)/shard_map/ppermute | solution.py:44
  77.3 13.3 %concatenate.103 = bf16[576,1664]{1,0:T(8,128)(2,1)} concatenate(bf16[9,1664]{1,0:T(8,128)(2,1)S(1)} %pad_maximum_fusion.12, bf16[9,1664]{1,0:T(8,128)(2,1)S(1)} %collective-permute-done, bf16[9,1664]{1,0:T(8,128)(2,1)S(1)} %collective-permute-done.1, bf16[9,1664]{1,0:T(8,128)(2,1)S(1)} %collective-permute-done.2, bf16[36,1664]{1,0:T(8,128)(2,1)S(1)} %collective-permute-done.3, ...), dimensions={0} | concatenate | bytes 3833856 | tf_op jit(solution)/shard_map/concatenate | solution.py:104
  96.8 20.9 %concatenate.104 = bf16[1152,1664]{1,0:T(8,128)(2,1)} concatenate(bf16[9,1664]{1,0:T(8,128)(2,1)S(1)} %pad_maximum_fusion.12, bf16[9,1664]{1,0:T(8,128)(2,1)} %copy-done.32, bf16[9,1664]{1,0:T(8,128)(2,1)} %copy-done.31, bf16[9,1664]{1,0:T(8,128)(2,1)S(1)} %collective-permute-done.2, bf16[36,1664]{1,0:T(8,128)(2,1)} %copy-done.26, bf16[36,1664]{1,0:T(8,128)(2,1)S(1)} %collective-permute-done.4, ...), dimensions={0} | concatenate | bytes 7667712 | tf_op jit(solution)/shard_map/concatenate | solution.py:105
  137.1 7.0 %collective-permute-done.11 = bf16[256,512]{1,0:T(8,128)(2,1)S(1)} collective-permute-done((bf16[256,512]{1,0:T(8,128)(2,1)S(1)}, bf16[256,512]{1,0:T(8,128)(2,1)S(1)}, u32[]{:S(2)}, u32[]{:S(2)}) %collective-permute-start.11) | collective-permute-done | bytes 262176 | tf_op jit(solution)/shard_map/ppermute | solution.py:44
  148.3 4.9 %collective-permute-start.14 = (bf16[1024,512]{1,0:T(8,128)(2,1)}, bf16[1024,512]{1,0:T(8,128)(2,1)}, u32[]{:S(2)}, u32[]{:S(2)}) collective-permute-start(bf16[1024,512]{1,0:T(8,128)(2,1)} %get-tuple-element.76), channel_id=1, source_target_pairs={{0,1},{1,0},{2,3},{3,2},{4,5},{5,4},{6,7},{7,6},{8,9},{9,8},{10,11... | collective-permute-start | bytes 3145736 | tf_op jit(solution)/shard_map/ppermute | solution.py:44
  170.6 8.2 %collective-permute-done.17 = bf16[128,1152]{1,0:T(8,128)(2,1)S(1)} collective-permute-done((bf16[128,1152]{1,0:T(8,128)(2,1)S(1)}, bf16[128,1152]{1,0:T(8,128)(2,1)S(1)}, u32[]{:S(2)}, u32[]{:S(2)}) %collective-permute-start.17) | collective-permute-done | bytes 294944 | tf_op jit(solution)/shard_map/ppermute | solution.py:44
  182.0 3.8 collective-permute-done.15
  201.1 6.9 %collective-permute-done.20 = bf16[128,1152]{1,0:T(8,128)(2,1)S(1)} collective-permute-done((bf16[128,1152]{1,0:T(8,128)(2,1)S(1)}, bf16[128,1152]{1,0:T(8,128)(2,1)S(1)}, u32[]{:S(2)}, u32[]{:S(2)}) %collective-permute-start.20) | collective-permute-done | bytes 294944 | tf_op jit(solution)/shard_map/ppermute | solution.py:44
  209.5 7.1 %collective-permute-done.21 = bf16[128,1152]{1,0:T(8,128)(2,1)S(1)} collective-permute-done((bf16[128,1152]{1,0:T(8,128)(2,1)S(1)}, bf16[128,1152]{1,0:T(8,128)(2,1)S(1)}, u32[]{:S(2)}, u32[]{:S(2)}) %collective-permute-start.21) | collective-permute-done | bytes 294944 | tf_op jit(solution)/shard_map/ppermute | solution.py:44
  220.5 7.9 %collective-permute-done.25 = bf16[128,1152]{1,0:T(8,128)(2,1)S(1)} collective-permute-done((bf16[128,1152]{1,0:T(8,128)(2,1)S(1)}, bf16[128,1152]{1,0:T(8,128)(2,1)S(1)}, u32[]{:S(2)}, u32[]{:S(2)}) %collective-permute-start.25) | collective-permute-done | bytes 294944 | tf_op jit(solution)/shard_map/ppermute | solution.py:44
  245.2 4.6 %convolution_convert_fusion = bf16[1152,1792]{1,0:T(8,128)(2,1)S(1)} fusion(bf16[1024,1152]{1,0:T(8,128)(2,1)S(1)} %constant_dynamic-update-slice_fusion.12, bf16[512,896]{1,0:T(8,128)(2,1)S(1)} %get-tuple-element.41, bf16[512,896]{1,0:T(8,128)(2,1)S(1)} %get-tuple-element.40, bf16[512,896]{1,0:T(8,128)(2,1)S(1)} %get-tuple-element.39, ...), kind=kOutput, calls=%fused_computation.2 | convolution fusion | flops 4244602880 | bytes 10158080 | tf_op jit(solution)/shard_map/dot_general | solution.py:63
  259.3 3.7 fusion.1
  267.4 7.4 %collective-permute-done.29 = bf16[128,1152]{1,0:T(8,128)(2,1)} collective-permute-done((bf16[128,1152]{1,0:T(8,128)(2,1)}, bf16[128,1152]{1,0:T(8,128)(2,1)}, u32[]{:S(2)}, u32[]{:S(2)}) %collective-permute-start.29) | collective-permute-done | bytes 294944 | tf_op jit(solution)/shard_map/ppermute | solution.py:44
  304.2 5.7 %collective-permute-done.32 = bf16[256,512]{1,0:T(8,128)(2,1)} collective-permute-done((bf16[256,512]{1,0:T(8,128)(2,1)}, bf16[256,512]{1,0:T(8,128)(2,1)}, u32[]{:S(2)}, u32[]{:S(2)}) %collective-permute-start.32) | collective-permute-done | bytes 262176 | tf_op jit(solution)/shard_map/ppermute | solution.py:44
  312.1 6.1 %collective-permute-done.33 = bf16[256,512]{1,0:T(8,128)(2,1)} collective-permute-done((bf16[256,512]{1,0:T(8,128)(2,1)}, bf16[256,512]{1,0:T(8,128)(2,1)}, u32[]{:S(2)}, u32[]{:S(2)}) %collective-permute-start.33) | collective-permute-done | bytes 262176 | tf_op jit(solution)/shard_map/ppermute | solution.py:44
  322.4 4.0 collective-permute-done.35
  341.0 13.5 %collective-permute-done.47 = bf16[128,1152]{1,0:T(8,128)(2,1)S(1)} collective-permute-done((bf16[128,1152]{1,0:T(8,128)(2,1)S(1)}, bf16[128,1152]{1,0:T(8,128)(2,1)S(1)}, u32[]{:S(2)}, u32[]{:S(2)}) %collective-permute-start.47) | collective-permute-done | bytes 294944 | tf_op jit(solution)/shard_map/ppermute | solution.py:44
  363.7 7.4 %collective-permute-done.37 = bf16[144,1664]{1,0:T(8,128)(2,1)S(1)} collective-permute-done((bf16[144,1664]{1,0:T(8,128)(2,1)S(1)}, bf16[144,1664]{1,0:T(8,128)(2,1)S(1)}, u32[]{:S(2)}, u32[]{:S(2)}) %collective-permute-start.37) | collective-permute-done | bytes 479264 | tf_op jit(solution)/shard_map/ppermute | solution.py:44
  371.1 10.8 %collective-permute-done.38 = bf16[144,1664]{1,0:T(8,128)(2,1)S(1)} collective-permute-done((bf16[144,1664]{1,0:T(8,128)(2,1)S(1)}, bf16[144,1664]{1,0:T(8,128)(2,1)S(1)}, u32[]{:S(2)}, u32[]{:S(2)}) %collective-permute-start.38) | collective-permute-done | bytes 479264 | tf_op jit(solution)/shard_map/ppermute | solution.py:44
  402.9 8.4 %all-to-all-start.1 = ((bf16[8,9,1792]{2,1,0:T(8,128)(2,1)}), bf16[8,9,1792]{2,1,0:T(8,128)(2,1)S(1)}, u32[]{:S(2)}, u32[]{:S(2)}) async-start(bf16[8,9,1792]{2,1,0:T(8,128)(2,1)} %reshape.751), calls=%async_computation.2 | async-start | bytes 917504 | tf_op jit(solution)/shard_map/all_to_all | solution.py:288
  412.9 7.2 %all-to-all-done.1 = bf16[8,9,1792]{2,1,0:T(8,128)(2,1)S(1)} async-done(((bf16[8,9,1792]{2,1,0:T(8,128)(2,1)}), bf16[8,9,1792]{2,1,0:T(8,128)(2,1)S(1)}, u32[]{:S(2)}, u32[]{:S(2)}) %all-to-all-start.1) | async-done | bytes 258080 | tf_op jit(solution)/shard_map/all_to_all | solution.py:288
  (430 shorter events, 215.1 us)
Async XLA Ops:
  7.2 157.9 %all-gather.3.cloned.1.call-start = ((), (), s32[]{:S(2)}) async-start(), calls=%async_computation.4 | async-start | bytes 11698176 | tf_op jit(solution)/shard_map/all_gather | solution.py:174
  30.1 370.9 %reduce-scatter.2.cloned.1.call-start = ((), (), s32[]{:S(2)}) async-start(), calls=%async_computation.3 | async-start | bytes 7798784 | tf_op jit(solution)/shard_map/reduce_scatter | solution.py:284
  53.2 15.5 %collective-permute-start.8 = (bf16[144,1664]{1,0:T(8,128)(2,1)S(1)}, bf16[144,1664]{1,0:T(8,128)(2,1)S(1)}, u32[]{:S(2)}, u32[]{:S(2)}) collective-permute-start(bf16[144,1664]{1,0:T(8,128)(2,1)S(1)} %concatenate.102), channel_id=1, source_target_pairs={{0,2},{1,3},{2,4},{3,5},{4,6},{5,7},{6,0},{7,1},{8,10},{9,11},{10,... | collective-permute-start | bytes 1437704 | tf_op jit(solution)/shard_map/ppermute | solution.py:44
  53.3 16.1 %collective-permute-start.7 = (bf16[144,1664]{1,0:T(8,128)(2,1)S(1)}, bf16[144,1664]{1,0:T(8,128)(2,1)S(1)}, u32[]{:S(2)}, u32[]{:S(2)}) collective-permute-start(bf16[144,1664]{1,0:T(8,128)(2,1)S(1)} %concatenate.102), channel_id=1, source_target_pairs={{0,4},{1,5},{2,6},{3,7},{4,0},{5,1},{6,2},{7,3},{8,12},{9,13},{10,... | collective-permute-start | bytes 1437704 | tf_op jit(solution)/shard_map/ppermute | solution.py:44
  53.8 22.8 %collective-permute-start.6 = (bf16[144,1664]{1,0:T(8,128)(2,1)S(1)}, bf16[144,1664]{1,0:T(8,128)(2,1)S(1)}, u32[]{:S(2)}, u32[]{:S(2)}) collective-permute-start(bf16[144,1664]{1,0:T(8,128)(2,1)S(1)} %concatenate.102), channel_id=1, source_target_pairs={{0,6},{1,7},{2,0},{3,1},{4,2},{5,3},{6,4},{7,5},{8,14},{9,15},{10,... | collective-permute-start | bytes 1437704 | tf_op jit(solution)/shard_map/ppermute | solution.py:44
  133.1 11.8 %collective-permute-start.12 = (bf16[256,512]{1,0:T(8,128)(2,1)S(1)}, bf16[256,512]{1,0:T(8,128)(2,1)S(1)}, u32[]{:S(2)}, u32[]{:S(2)}) collective-permute-start(bf16[256,512]{1,0:T(8,128)(2,1)S(1)} %pad_maximum_fusion.6), channel_id=1, source_target_pairs={{0,6},{1,7},{2,0},{3,1},{4,2},{5,3},{6,4},{7,5},{8,14},{9,15},{10,... | collective-permute-start | bytes 786440 | tf_op jit(solution)/shard_map/ppermute | solution.py:44
  135.2 12.4 %collective-permute-start.13 = (bf16[256,512]{1,0:T(8,128)(2,1)S(1)}, bf16[256,512]{1,0:T(8,128)(2,1)S(1)}, u32[]{:S(2)}, u32[]{:S(2)}) collective-permute-start(bf16[256,512]{1,0:T(8,128)(2,1)S(1)} %pad_maximum_fusion.6), channel_id=1, source_target_pairs={{0,4},{1,5},{2,6},{3,7},{4,0},{5,1},{6,2},{7,3},{8,12},{9,13},{10,... | collective-permute-start | bytes 786440 | tf_op jit(solution)/shard_map/ppermute | solution.py:44
  169.0 9.8 %collective-permute-start.17 = (bf16[128,1152]{1,0:T(8,128)(2,1)S(1)}, bf16[128,1152]{1,0:T(8,128)(2,1)S(1)}, u32[]{:S(2)}, u32[]{:S(2)}) collective-permute-start(bf16[128,1152]{1,0:T(8,128)(2,1)S(1)} %get-tuple-element.30), channel_id=1, source_target_pairs={{0,4},{1,5},{2,6},{3,7},{4,0},{5,1},{6,2},{7,3},{8,12},{9,13},{10,... | collective-permute-start | bytes 884744 | tf_op jit(solution)/shard_map/ppermute | solution.py:44
  169.1 13.0 %collective-permute-start.16 = (bf16[128,1152]{1,0:T(8,128)(2,1)S(1)}, bf16[128,1152]{1,0:T(8,128)(2,1)S(1)}, u32[]{:S(2)}, u32[]{:S(2)}) collective-permute-start(bf16[128,1152]{1,0:T(8,128)(2,1)S(1)} %get-tuple-element.30), channel_id=1, source_target_pairs={{0,6},{1,7},{2,0},{3,1},{4,2},{5,3},{6,4},{7,5},{8,14},{9,15},{10,... | collective-permute-start | bytes 884744 | tf_op jit(solution)/shard_map/ppermute | solution.py:44
  169.2 16.7 %collective-permute-start.15 = (bf16[128,1152]{1,0:T(8,128)(2,1)S(1)}, bf16[128,1152]{1,0:T(8,128)(2,1)S(1)}, u32[]{:S(2)}, u32[]{:S(2)}) collective-permute-start(bf16[128,1152]{1,0:T(8,128)(2,1)S(1)} %get-tuple-element.30), channel_id=1, source_target_pairs={{0,2},{1,3},{2,4},{3,5},{4,6},{5,7},{6,0},{7,1},{8,10},{9,11},{10,... | collective-permute-start | bytes 884744 | tf_op jit(solution)/shard_map/ppermute | solution.py:44
  199.9 16.8 %collective-permute-start.21 = (bf16[128,1152]{1,0:T(8,128)(2,1)S(1)}, bf16[128,1152]{1,0:T(8,128)(2,1)S(1)}, u32[]{:S(2)}, u32[]{:S(2)}) collective-permute-start(bf16[128,1152]{1,0:T(8,128)(2,1)S(1)} %get-tuple-element.55), channel_id=1, source_target_pairs={{0,2},{1,3},{2,4},{3,5},{4,6},{5,7},{6,0},{7,1},{8,10},{9,11},{10,... | collective-permute-start | bytes 884744 | tf_op jit(solution)/shard_map/ppermute | solution.py:44
  218.7 13.2 %collective-permute-start.24 = (bf16[128,1152]{1,0:T(8,128)(2,1)S(1)}, bf16[128,1152]{1,0:T(8,128)(2,1)S(1)}, u32[]{:S(2)}, u32[]{:S(2)}) collective-permute-start(bf16[128,1152]{1,0:T(8,128)(2,1)S(1)} %get-tuple-element.32), channel_id=1, source_target_pairs={{0,6},{1,7},{2,0},{3,1},{4,2},{5,3},{6,4},{7,5},{8,14},{9,15},{10,... | collective-permute-start | bytes 884744 | tf_op jit(solution)/shard_map/ppermute | solution.py:44
  218.9 16.6 %collective-permute-start.23 = (bf16[128,1152]{1,0:T(8,128)(2,1)S(1)}, bf16[128,1152]{1,0:T(8,128)(2,1)S(1)}, u32[]{:S(2)}, u32[]{:S(2)}) collective-permute-start(bf16[128,1152]{1,0:T(8,128)(2,1)S(1)} %get-tuple-element.32), channel_id=1, source_target_pairs={{0,2},{1,3},{2,4},{3,5},{4,6},{5,7},{6,0},{7,1},{8,10},{9,11},{10,... | collective-permute-start | bytes 884744 | tf_op jit(solution)/shard_map/ppermute | solution.py:44
  257.8 17.1 %collective-permute-start.29 = (bf16[128,1152]{1,0:T(8,128)(2,1)}, bf16[128,1152]{1,0:T(8,128)(2,1)}, u32[]{:S(2)}, u32[]{:S(2)}) collective-permute-start(bf16[128,1152]{1,0:T(8,128)(2,1)} %get-tuple-element.52), channel_id=1, source_target_pairs={{0,2},{1,3},{2,4},{3,5},{4,6},{5,7},{6,0},{7,1},{8,10},{9,11},{10,... | collective-permute-start | bytes 884744 | tf_op jit(solution)/shard_map/ppermute | solution.py:44
  298.4 38.2 %collective-permute-start.46 = (bf16[512,1152]{1,0:T(8,128)(2,1)}, bf16[512,1152]{1,0:T(8,128)(2,1)}, u32[]{:S(2)}, u32[]{:S(2)}) collective-permute-start(bf16[512,1152]{1,0:T(8,128)(2,1)} %slice.387), channel_id=1, source_target_pairs={{0,1},{1,0},{2,3},{3,2},{4,5},{5,4},{6,7},{7,6},{8,9},{9,8},{10,11... | collective-permute-start | bytes 3538952 | tf_op jit(solution)/shard_map/ppermute | solution.py:44
  302.5 15.6 %collective-permute-start.33 = (bf16[256,512]{1,0:T(8,128)(2,1)}, bf16[256,512]{1,0:T(8,128)(2,1)}, u32[]{:S(2)}, u32[]{:S(2)}) collective-permute-start(bf16[256,512]{1,0:T(8,128)(2,1)} %get-tuple-element.58), channel_id=1, source_target_pairs={{0,2},{1,3},{2,4},{3,5},{4,6},{5,7},{6,0},{7,1},{8,10},{9,11},{10,... | collective-permute-start | bytes 786440 | tf_op jit(solution)/shard_map/ppermute | solution.py:44
  335.4 23.0 %collective-permute-start.36 = (bf16[576,1664]{1,0:T(8,128)(2,1)S(1)}, bf16[576,1664]{1,0:T(8,128)(2,1)S(1)}, u32[]{:S(2)}, u32[]{:S(2)}) collective-permute-start(bf16[576,1664]{1,0:T(8,128)(2,1)S(1)} %pad_maximum_fusion), channel_id=1, source_target_pairs={{0,1},{1,0},{2,3},{3,2},{4,5},{5,4},{6,7},{7,6},{8,9},{9,8},{10,11... | collective-permute-start | bytes 5750792 | tf_op jit(solution)/shard_map/ppermute | solution.py:44
  338.2 16.2 %collective-permute-start.47 = (bf16[128,1152]{1,0:T(8,128)(2,1)S(1)}, bf16[128,1152]{1,0:T(8,128)(2,1)S(1)}, u32[]{:S(2)}, u32[]{:S(2)}) collective-permute-start(bf16[128,1152]{1,0:T(8,128)(2,1)S(1)} %get-tuple-element.47), channel_id=1, source_target_pairs={{0,2},{1,3},{2,4},{3,5},{4,6},{5,7},{6,0},{7,1},{8,10},{9,11},{10,... | collective-permute-start | bytes 884744 | tf_op jit(solution)/shard_map/ppermute | solution.py:44
  338.3 16.1 %collective-permute-start.49 = (bf16[128,1152]{1,0:T(8,128)(2,1)S(1)}, bf16[128,1152]{1,0:T(8,128)(2,1)S(1)}, u32[]{:S(2)}, u32[]{:S(2)}) collective-permute-start(bf16[128,1152]{1,0:T(8,128)(2,1)S(1)} %get-tuple-element.48), channel_id=1, source_target_pairs={{0,6},{1,7},{2,0},{3,1},{4,2},{5,3},{6,4},{7,5},{8,14},{9,15},{10,... | collective-permute-start | bytes 884744 | tf_op jit(solution)/shard_map/ppermute | solution.py:44
  341.0 13.5 %collective-permute-start.48 = (bf16[128,1152]{1,0:T(8,128)(2,1)S(1)}, bf16[128,1152]{1,0:T(8,128)(2,1)S(1)}, u32[]{:S(2)}, u32[]{:S(2)}) collective-permute-start(bf16[128,1152]{1,0:T(8,128)(2,1)S(1)} %get-tuple-element.49), channel_id=1, source_target_pairs={{0,4},{1,5},{2,6},{3,7},{4,0},{5,1},{6,2},{7,3},{8,12},{9,13},{10,... | collective-permute-start | bytes 884744 | tf_op jit(solution)/shard_map/ppermute | solution.py:44
  359.0 12.1 %collective-permute-start.37 = (bf16[144,1664]{1,0:T(8,128)(2,1)S(1)}, bf16[144,1664]{1,0:T(8,128)(2,1)S(1)}, u32[]{:S(2)}, u32[]{:S(2)}) collective-permute-start(bf16[144,1664]{1,0:T(8,128)(2,1)S(1)} %get-tuple-element.42), channel_id=1, source_target_pairs={{0,2},{1,3},{2,4},{3,5},{4,6},{5,7},{6,0},{7,1},{8,10},{9,11},{10,... | collective-permute-start | bytes 1437704 | tf_op jit(solution)/shard_map/ppermute | solution.py:44
  359.7 11.5 %collective-permute-start.39 = (bf16[144,1664]{1,0:T(8,128)(2,1)S(1)}, bf16[144,1664]{1,0:T(8,128)(2,1)S(1)}, u32[]{:S(2)}, u32[]{:S(2)}) collective-permute-start(bf16[144,1664]{1,0:T(8,128)(2,1)S(1)} %get-tuple-element.43), channel_id=1, source_target_pairs={{0,6},{1,7},{2,0},{3,1},{4,2},{5,3},{6,4},{7,5},{8,14},{9,15},{10,... | collective-permute-start | bytes 1437704 | tf_op jit(solution)/shard_map/ppermute | solution.py:44
  361.8 20.2 %collective-permute-start.38 = (bf16[144,1664]{1,0:T(8,128)(2,1)S(1)}, bf16[144,1664]{1,0:T(8,128)(2,1)S(1)}, u32[]{:S(2)}, u32[]{:S(2)}) collective-permute-start(bf16[144,1664]{1,0:T(8,128)(2,1)S(1)} %get-tuple-element.44), channel_id=1, source_target_pairs={{0,4},{1,5},{2,6},{3,7},{4,0},{5,1},{6,2},{7,3},{8,12},{9,13},{10,... | collective-permute-start | bytes 1437704 | tf_op jit(solution)/shard_map/ppermute | solution.py:44
  402.9 17.2 %all-to-all-start.1 = ((bf16[8,9,1792]{2,1,0:T(8,128)(2,1)}), bf16[8,9,1792]{2,1,0:T(8,128)(2,1)S(1)}, u32[]{:S(2)}, u32[]{:S(2)}) async-start(bf16[8,9,1792]{2,1,0:T(8,128)(2,1)} %reshape.751), calls=%async_computation.2 | async-start | bytes 917504 | tf_op jit(solution)/shard_map/all_to_all | solution.py:288
  (110 other events, 765.3 us)
Sparse Core Ops, SparseCore 0:
  30.2 85.1 all-gather.2
  263.2 83.6 reduce-scatter.1
